TPU v7x, 32 devices: a whole 2x2x4 slice. The times are simulated.
32 devices in a mesh: wind: 4 (over z), state: 8 (over y, x, core).
Axes of the slice: x: 2, y: 2, z: 4, core: 2. Of those that a mesh axis runs over, the one named last changes fastest.
Arguments:
- value_next: float32 [128, 16, 256, 256], P('wind', None, 'state'), may hold values from -6 to 6
- density: float32 [128, 16, 256, 256], P('wind', None, 'state'), may hold values from 0.1 to 2
- price: float32 [128, 16], P('wind'), may hold values from -4 to 4
- wind_rate: float32 [128, 16], P('wind'), may hold values from 0.05 to 0.5
- tank_inverse: float32 [256, 256], replicated, may hold values from -0.5 to 1.5
- soc_inverse: float32 [256, 256], replicated, may hold values from -0.5 to 1.5
Outputs:
- value: float32 [128, 16, 256, 256], P('wind', None, 'state')
- density_next: float32 [128, 16, 256, 256], P('wind', None, 'state')
All inputs are finite; a program needn't handle non-finite values.
Results may differ from a plain program's by a relative error of at most 0.0001.
Values sent between devices are 32-bit elements; how exact they have to be, the bound alone decides.
No kernel may reach another device: no remote copies, remote signals or barrier semaphores. Data moves between devices by JAX's collectives and lax.ppermute only.
A program may use at most 320 MiB of HBM per device.

v0:
```python
import jax
import jax.numpy as jnp
from jax import lax
from jax.sharding import PartitionSpec as P

ITERS = 4


step_size = 0.25
control_bound = 2.0
control_cost = 1.0
tank_spread = 0.3


def extended(cells, sides, width):
    for axis, dim in sides:
        count = lax.axis_size(axis)
        ends = count - 1
        head = lax.slice_in_dim(cells, 0, width, axis=dim)
        tail = lax.slice_in_dim(cells, cells.shape[dim] - width, cells.shape[dim], axis=dim)
        cells = jnp.concatenate(
            [
                lax.ppermute(tail, axis, [(i, (i + 1) % count) for i in range(ends)]),
                cells,
                lax.ppermute(head, axis, [((i + 1) % count, i) for i in range(ends)]),
            ],
            axis=dim,
        )
    return cells


def control_law(slope, price):
    shifted = slope + price[:, :, None, None]
    action = -control_bound * jnp.tanh(shifted / (control_cost * control_bound))
    hamilton = action * shifted + 0.5 * control_cost * action * action
    return (action, hamilton)


def value_rims(current):
    return extended(current, (("wind", 0), ("state", 2)), 1)


def regroup(block):
    return jnp.swapaxes(block, 2, 3)


def on_device(value_next, density, price, wind_rate, tank_inverse, soc_inverse):
    rates = wind_rate[:, :, None, None]
    current = value_next
    for sweep in range(ITERS):
        padded = value_rims(current)
        slope = 0.5 * (padded[1:-1, :, 2:] - padded[1:-1, :, :-2])
        action, hamilton = control_law(slope, price)
        couple = rates * (padded[2:, :, 1:-1] + padded[:-2, :, 1:-1] - 2.0 * current)
        source = value_next + step_size * (hamilton + couple)
        current = jnp.einsum(
            "wrsk,tk->wrst",
            source,
            tank_inverse,
            precision=lax.Precision.HIGHEST,
            preferred_element_type=jnp.float32,
        )
    moved = regroup(lax.all_to_all(current, "state", split_axis=3, concat_axis=2, tiled=True))
    edged = jnp.pad(moved, ((0, 0), (0, 0), (0, 0), (1, 1)))
    slope = 0.5 * (edged[:, :, :, 2:] - edged[:, :, :, :-2])
    drift, hamilton = control_law(slope, price)
    flux_edged = jnp.pad(drift * density, ((0, 0), (0, 0), (0, 0), (1, 1)))
    spread = 0.5 * (flux_edged[:, :, :, 2:] - flux_edged[:, :, :, :-2])
    padded = extended(density, (("wind", 0), ("state", 2)), 1)
    tank_term = tank_spread * (padded[1:-1, :, 2:] + padded[1:-1, :, :-2] - 2.0 * density)
    wind_term = rates * (padded[2:, :, 1:-1] + padded[:-2, :, 1:-1] - 2.0 * density)
    source = density + step_size * (tank_term + wind_term - spread)
    density_next = jnp.einsum(
        "wrks,ts->wrkt",
        source,
        soc_inverse,
        precision=lax.Precision.HIGHEST,
        preferred_element_type=jnp.float32,
    )
    return (current, density_next)


def solution(mesh):
    placed = (
        P("wind", None, "state", None),
        P("wind", None, "state", None),
        P("wind", None),
        P("wind", None),
        P(),
        P(),
    )
    return jax.shard_map(
        on_device,
        mesh=mesh,
        in_specs=placed,
        out_specs=(P("wind", None, "state", None), P("wind", None, "state", None)),
        check_vma=False,
    )
```

profile of v0, /device:TPU:25, one launch (start us, length us, event | category | flops | bytes accessed | tf_op | source)
XLA Modules:
  0.0 904.7 jit_solution(8132402842203579111)
XLA Ops:
  7.3 9.4 %collective-permute-done = f32[1,16,32,256]{3,2,1,0:T(8,128)S(1)} collective-permute-done((f32[1,16,32,256]{3,2,1,0:T(8,128)S(1)}, f32[1,16,32,256]{3,2,1,0:T(8,128)S(1)}, u32[]{:S(2)}, u32[]{:S(2)}) %collective-permute-start) | collective-permute-done | bytes 524320 | tf_op jit(solution)/shard_map/ppermute | solution.py:23
  16.7 7.7 constant_dynamic-update-slice_fusion.1
  30.6 4.5 collective-permute-start.3
  41.6 39.0 %fusion.73 = f32[32,16,32,256]{3,2,1,0:T(8,128)} fusion(f32[32,16,32,256]{3,2,1,0:T(8,128)} %param.6, f32[1,16,32,256]{3,2,1,0:T(8,128)S(1)} %collective-permute-done, f32[1,16,32,256]{3,2,1,0:T(8,128)S(1)} %collective-permute-done.1, f32[34,16,32,256]{3,2,1,0:T(8,128)} %copy-done.5, f32[34,16,1,256]{3,2,1,0:T(1,128)} %collective-permute-done.3, ...), kind=kOutput, calls=%fused_computation.101 | convolution fusion | flops 12964593664 | bytes 53809152 | tf_op jit(solution)/shard_map/wrsk,tk->wrst/dot_general | solution.py:56
  87.9 4.5 collective-permute-done.4
  100.0 9.2 %collective-permute-start.7 = (f32[34,16,1,256]{3,2,1,0:T(1,128)S(1)}, f32[34,16,1,256]{3,2,1,0:T(1,128)S(1)}, u32[]{:S(2)}, u32[]{:S(2)}) collective-permute-start(f32[34,16,1,256]{3,2,1,0:T(1,128)S(1)} %get-tuple-element.9), channel_id=1, source_target_pairs={{0,1},{1,2},{2,3},{3,4},{4,5},{5,6},{6,7},{8,9},{9,10},{10,11},{11... | collective-permute-start | bytes 1671176 | tf_op jit(solution)/shard_map/ppermute | solution.py:23
  109.3 8.3 collective-permute-done.6
  117.6 30.1 %fusion.60 = f32[32,16,32,256]{3,2,1,0:T(8,128)} fusion(f32[32,16,32,256]{3,2,1,0:T(8,128)} %param.6, f32[32,16,32,256]{3,2,1,0:T(8,128)S(1)} %copy-done.2, f32[1,16,32,256]{3,2,1,0:T(8,128)S(1)} %collective-permute-done.4, f32[1,16,32,256]{3,2,1,0:T(8,128)S(1)} %collective-permute-done.5, f32[34,16,1,256]{3,2,1,0:T(1,128)S(1)} %collective-permute-done.7, ...), kind=kOutput, calls=%fused_computation.81 | convolution fusion | flops 12981370880 | bytes 52760576 | tf_op jit(solution)/shard_map/wrsk,tk->wrst/dot_general | solution.py:56
  150.8 5.4 collective-permute-start.9
  168.1 7.6 collective-permute-start.11
  175.7 5.7 collective-permute-done.10
  182.2 30.1 %fusion.47 = f32[32,16,32,256]{3,2,1,0:T(8,128)} fusion(f32[32,16,32,256]{3,2,1,0:T(8,128)} %param.6, f32[32,16,32,256]{3,2,1,0:T(8,128)S(1)} %copy-done.3, f32[1,16,32,256]{3,2,1,0:T(8,128)S(1)} %collective-permute-done.8, f32[1,16,32,256]{3,2,1,0:T(8,128)S(1)} %collective-permute-done.9, f32[34,16,1,256]{3,2,1,0:T(1,128)S(1)} %collective-permute-done.11, ...), kind=kOutput, calls=%fused_computation.61 | convolution fusion | flops 12981370880 | bytes 52760576 | tf_op jit(solution)/shard_map/wrsk,tk->wrst/dot_general | solution.py:56
  215.3 5.2 collective-permute-start.13
  220.5 4.3 collective-permute-done.12
  232.6 7.0 collective-permute-start.15
  239.6 5.3 collective-permute-done.14
  246.1 30.1 %fusion.34 = f32[32,16,32,256]{3,2,1,0:T(8,128)} fusion(f32[32,16,32,256]{3,2,1,0:T(8,128)} %param.6, f32[32,16,32,256]{3,2,1,0:T(8,128)S(1)} %copy-done.4, f32[1,16,32,256]{3,2,1,0:T(8,128)S(1)} %collective-permute-done.12, f32[1,16,32,256]{3,2,1,0:T(8,128)S(1)} %collective-permute-done.13, f32[34,16,1,256]{3,2,1,0:T(1,128)S(1)} %collective-permute-done.15, ...), kind=kOutput, calls=%fused_computation.41 | convolution fusion | flops 12981370880 | bytes 52760576 | tf_op jit(solution)/shard_map/wrsk,tk->wrst/dot_general | solution.py:56
  276.2 50.4 %copy.13 = f32[32,16,32,256]{2,1,0,3:T(8,128)} copy(f32[32,16,32,256]{3,2,1,0:T(8,128)} %fusion.34) | data formatting | bytes 33554432 | tf_op jit(solution)/shard_map/wrsk,tk->wrst/dot_general | solution.py:56
  326.6 66.9 %reshape.8 = f32[8,1,524288]{2,1,0:T(1,128)} reshape(f32[256,32,16,32]{3,2,1,0:T(8,128)} %bitcast.24) | data formatting | bytes 33554432
  393.5 16.0 %all-to-all-start = ((f32[8,1,524288]{2,1,0:T(1,128)}), f32[8,1,524288]{2,1,0:T(1,128)}, u32[]{:S(2)}, u32[]{:S(2)}) async-start(f32[8,1,524288]{2,1,0:T(1,128)} %reshape.8), calls=%async_computation | async-start | bytes 33554432 | tf_op jit(solution)/shard_map/all_to_all | solution.py:63
  412.1 4.8 collective-permute-start.17
  416.8 10.4 %collective-permute-done.16 = f32[1,16,32,256]{3,2,1,0:T(8,128)S(1)} collective-permute-done((f32[1,16,32,256]{3,2,1,0:T(8,128)S(1)}, f32[1,16,32,256]{3,2,1,0:T(8,128)S(1)}, u32[]{:S(2)}, u32[]{:S(2)}) %collective-permute-start.16) | collective-permute-done | bytes 524320 | tf_op jit(solution)/shard_map/ppermute | solution.py:23
  428.1 161.9 %all-to-all-done = f32[8,1,524288]{2,1,0:T(1,128)} async-done(((f32[8,1,524288]{2,1,0:T(1,128)}), f32[8,1,524288]{2,1,0:T(1,128)}, u32[]{:S(2)}, u32[]{:S(2)}) %all-to-all-start) | async-done | bytes 16777248 | tf_op jit(solution)/shard_map/all_to_all | solution.py:63
  590.5 59.2 %reduce = f32[8,524288]{1,0:T(8,128)} reduce(f32[8,1,524288]{2,1,0:T(1,128)} %all-to-all-done, f32[]{:T(128)} %broadcast.123), dimensions={1}, to_apply=%all_to_all.13.reduce_sub_computation | reduce | bytes 33554436 | tf_op jit(solution)/shard_map/all_to_all | solution.py:63
  649.7 55.4 %reshape.9 = f32[256,32,16,32]{3,2,1,0:T(8,128)} reshape(f32[8,524288]{1,0:T(8,128)} %reduce) | data formatting | bytes 33554432
  705.1 56.7 %copy.18 = f32[32,16,32,8,32]{2,3,4,1,0:T(8,128)} copy(f32[32,16,32,8,32]{2,1,0,4,3:T(8,128)} %bitcast.2) | data formatting | bytes 33554432 | tf_op jit(solution)/shard_map/all_to_all | solution.py:63
  761.9 45.3 %all_to_all.16 = f32[32,16,256,32]{2,3,1,0:T(8,128)} reshape(f32[32,16,8,32,32]{3,2,4,1,0:T(8,128)} %bitcast.28) | data formatting | bytes 33554432 | tf_op jit(solution)/shard_map/all_to_all | solution.py:63
  807.2 30.8 %constant_dynamic-update-slice_fusion.4 = (f32[34,16,32,256]{3,2,1,0:T(8,128)}, f32[32,16,32,256]{3,2,1,0:T(8,128)}) fusion(f32[34,16,32,256]{3,2,1,0:T(8,128)} %constant_dynamic-update-slice_fusion.5, f32[32,16,32,256]{3,2,1,0:T(8,128)} %param.7, f32[32,16]{1,0:T(8,128)S(1)} %copy-done.7, f32[32,16,32,256]{3,2,1,0:T(8,128)} %bitcast.29), kind=kLoop, calls=%fused_computation.189 | loop fusion | flops 25165824 | bytes 67110912
  838.8 4.6 fusion.180
  843.5 5.5 collective-permute-start.18
  851.0 7.8 collective-permute-done.18
  858.8 45.4 %fusion.12 = f32[32,16,32,256]{3,2,1,0:T(8,128)} fusion(f32[32,16,32,256]{3,2,1,0:T(8,128)} %param.7, f32[32,16,32,256]{3,2,1,0:T(8,128)} %get-tuple-element.13, f32[1,16,32,256]{3,2,1,0:T(8,128)S(1)} %collective-permute-done.16, f32[1,16,32,256]{3,2,1,0:T(8,128)S(1)} %collective-permute-done.17, ...), kind=kOutput, calls=%fused_computation.17 | convolution fusion | flops 12956205056 | bytes 70584320 | tf_op jit(solution)/shard_map/wrks,ts->wrkt/dot_general | solution.py:73
  (66 shorter events, 68.6 us)
Async XLA Ops:
  0.6 41.0 %copy-start = (f32[256,256]{1,0:T(8,128)S(1)}, f32[256,256]{1,0:T(8,128)}, u32[]{:S(2)}) copy-start(f32[256,256]{1,0:T(8,128)} %param.10) | copy-start | bytes 786436
  2.0 14.7 %collective-permute-start = (f32[1,16,32,256]{3,2,1,0:T(8,128)S(1)}, f32[1,16,32,256]{3,2,1,0:T(8,128)S(1)}, u32[]{:S(2)}, u32[]{:S(2)}) collective-permute-start(f32[1,16,32,256]{3,2,1,0:T(8,128)S(1)} %get-tuple-element.23), channel_id=1, source_target_pairs={{0,8},{8,16},{16,24},{1,9},{9,17},{17,25},{2,10},{10,18},{18,26},{... | collective-permute-start | bytes 1572872 | tf_op jit(solution)/shard_map/ppermute | solution.py:23
  3.3 21.1 %collective-permute-start.1 = (f32[1,16,32,256]{3,2,1,0:T(8,128)S(1)}, f32[1,16,32,256]{3,2,1,0:T(8,128)S(1)}, u32[]{:S(2)}, u32[]{:S(2)}) collective-permute-start(f32[1,16,32,256]{3,2,1,0:T(8,128)S(1)} %get-tuple-element.22), channel_id=1, source_target_pairs={{8,0},{16,8},{24,16},{9,1},{17,9},{25,17},{10,2},{18,10},{26,18},{... | collective-permute-start | bytes 1572872 | tf_op jit(solution)/shard_map/ppermute | solution.py:25
  16.7 18.5 %copy-start.11 = (f32[32,16]{0,1:T(8,128)S(1)}, f32[32,16]{0,1:T(8,128)}, u32[]{:S(2)}) copy-start(f32[32,16]{0,1:T(8,128)} %param.9) | copy-start | bytes 6148
  25.8 11.9 %collective-permute-start.2 = (f32[34,16,1,256]{3,2,1,0:T(1,128)S(1)}, f32[34,16,1,256]{3,2,1,0:T(1,128)S(1)}, u32[]{:S(2)}, u32[]{:S(2)}) collective-permute-start(f32[34,16,1,256]{3,2,1,0:T(1,128)S(1)} %get-tuple-element.10), channel_id=1, source_target_pairs={{1,0},{2,1},{3,2},{4,3},{5,4},{6,5},{7,6},{9,8},{10,9},{11,10},{12... | collective-permute-start | bytes 1671176 | tf_op jit(solution)/shard_map/ppermute | solution.py:25
  30.6 11.0 %collective-permute-start.3 = (f32[34,16,1,256]{3,2,1,0:T(1,128)S(1)}, f32[34,16,1,256]{3,2,1,0:T(1,128)}, u32[]{:S(2)}, u32[]{:S(2)}) collective-permute-start(f32[34,16,1,256]{3,2,1,0:T(1,128)S(1)} %get-tuple-element.11), channel_id=1, source_target_pairs={{0,1},{1,2},{2,3},{3,4},{4,5},{5,6},{6,7},{8,9},{9,10},{10,11},{11... | collective-permute-start | bytes 1671176 | tf_op jit(solution)/shard_map/ppermute | solution.py:23
  35.3 210.8 %copy-start.6 = (f32[32,16]{1,0:T(8,128)}, f32[32,16]{1,0:T(8,128)S(1)}, u32[]{:S(2)}) copy-start(f32[32,16]{1,0:T(8,128)S(1)} %copy.11) | copy-start | bytes 6148
  35.3 210.8 %copy-start.8 = (f32[32,16]{1,0:T(8,128)}, f32[32,16]{1,0:T(8,128)S(1)}, u32[]{:S(2)}) copy-start(f32[32,16]{1,0:T(8,128)S(1)} %copy.12) | copy-start | bytes 6148
  80.6 37.0 %copy-start.2 = (f32[32,16,32,256]{3,2,1,0:T(8,128)S(1)}, f32[32,16,32,256]{3,2,1,0:T(8,128)}, u32[]{:S(2)}) copy-start(f32[32,16,32,256]{3,2,1,0:T(8,128)} %fusion.73) | copy-start | bytes 50331652
  82.1 10.3 %collective-permute-start.4 = (f32[1,16,32,256]{3,2,1,0:T(8,128)S(1)}, f32[1,16,32,256]{3,2,1,0:T(8,128)S(1)}, u32[]{:S(2)}, u32[]{:S(2)}) collective-permute-start(f32[1,16,32,256]{3,2,1,0:T(8,128)S(1)} %get-tuple-element.21), channel_id=1, source_target_pairs={{0,8},{8,16},{16,24},{1,9},{9,17},{17,25},{2,10},{10,18},{18,26},{... | collective-permute-start | bytes 1572872 | tf_op jit(solution)/shard_map/ppermute | solution.py:23
  83.6 10.4 %collective-permute-start.5 = (f32[1,16,32,256]{3,2,1,0:T(8,128)S(1)}, f32[1,16,32,256]{3,2,1,0:T(8,128)S(1)}, u32[]{:S(2)}, u32[]{:S(2)}) collective-permute-start(f32[1,16,32,256]{3,2,1,0:T(8,128)S(1)} %get-tuple-element.20), channel_id=1, source_target_pairs={{8,0},{16,8},{24,16},{9,1},{17,9},{25,17},{10,2},{18,10},{26,18},{... | collective-permute-start | bytes 1572872 | tf_op jit(solution)/shard_map/ppermute | solution.py:25
  98.1 19.5 %collective-permute-start.6 = (f32[34,16,1,256]{3,2,1,0:T(1,128)S(1)}, f32[34,16,1,256]{3,2,1,0:T(1,128)S(1)}, u32[]{:S(2)}, u32[]{:S(2)}) collective-permute-start(f32[34,16,1,256]{3,2,1,0:T(1,128)S(1)} %get-tuple-element.8), channel_id=1, source_target_pairs={{1,0},{2,1},{3,2},{4,3},{5,4},{6,5},{7,6},{9,8},{10,9},{11,10},{12... | collective-permute-start | bytes 1671176 | tf_op jit(solution)/shard_map/ppermute | solution.py:25
  100.0 17.6 %collective-permute-start.7 = (f32[34,16,1,256]{3,2,1,0:T(1,128)S(1)}, f32[34,16,1,256]{3,2,1,0:T(1,128)S(1)}, u32[]{:S(2)}, u32[]{:S(2)}) collective-permute-start(f32[34,16,1,256]{3,2,1,0:T(1,128)S(1)} %get-tuple-element.9), channel_id=1, source_target_pairs={{0,1},{1,2},{2,3},{3,4},{4,5},{5,6},{6,7},{8,9},{9,10},{10,11},{11... | collective-permute-start | bytes 1671176 | tf_op jit(solution)/shard_map/ppermute | solution.py:23
  147.8 34.4 %copy-start.3 = (f32[32,16,32,256]{3,2,1,0:T(8,128)S(1)}, f32[32,16,32,256]{3,2,1,0:T(8,128)}, u32[]{:S(2)}) copy-start(f32[32,16,32,256]{3,2,1,0:T(8,128)} %fusion.60) | copy-start | bytes 50331652
  149.2 11.1 %collective-permute-start.8 = (f32[1,16,32,256]{3,2,1,0:T(8,128)S(1)}, f32[1,16,32,256]{3,2,1,0:T(8,128)S(1)}, u32[]{:S(2)}, u32[]{:S(2)}) collective-permute-start(f32[1,16,32,256]{3,2,1,0:T(8,128)S(1)} %get-tuple-element.19), channel_id=1, source_target_pairs={{0,8},{8,16},{16,24},{1,9},{9,17},{17,25},{2,10},{10,18},{18,26},{... | collective-permute-start | bytes 1572872 | tf_op jit(solution)/shard_map/ppermute | solution.py:23
  150.8 11.2 %collective-permute-start.9 = (f32[1,16,32,256]{3,2,1,0:T(8,128)S(1)}, f32[1,16,32,256]{3,2,1,0:T(8,128)S(1)}, u32[]{:S(2)}, u32[]{:S(2)}) collective-permute-start(f32[1,16,32,256]{3,2,1,0:T(8,128)S(1)} %get-tuple-element.18), channel_id=1, source_target_pairs={{8,0},{16,8},{24,16},{9,1},{17,9},{25,17},{10,2},{18,10},{26,18},{... | collective-permute-start | bytes 1572872 | tf_op jit(solution)/shard_map/ppermute | solution.py:25
  166.1 15.3 %collective-permute-start.10 = (f32[34,16,1,256]{3,2,1,0:T(1,128)S(1)}, f32[34,16,1,256]{3,2,1,0:T(1,128)S(1)}, u32[]{:S(2)}, u32[]{:S(2)}) collective-permute-start(f32[34,16,1,256]{3,2,1,0:T(1,128)S(1)} %get-tuple-element.6), channel_id=1, source_target_pairs={{1,0},{2,1},{3,2},{4,3},{5,4},{6,5},{7,6},{9,8},{10,9},{11,10},{12... | collective-permute-start | bytes 1671176 | tf_op jit(solution)/shard_map/ppermute | solution.py:25
  168.1 14.1 %collective-permute-start.11 = (f32[34,16,1,256]{3,2,1,0:T(1,128)S(1)}, f32[34,16,1,256]{3,2,1,0:T(1,128)S(1)}, u32[]{:S(2)}, u32[]{:S(2)}) collective-permute-start(f32[34,16,1,256]{3,2,1,0:T(1,128)S(1)} %get-tuple-element.7), channel_id=1, source_target_pairs={{0,1},{1,2},{2,3},{3,4},{4,5},{5,6},{6,7},{8,9},{9,10},{10,11},{11... | collective-permute-start | bytes 1671176 | tf_op jit(solution)/shard_map/ppermute | solution.py:23
  212.3 33.8 %copy-start.4 = (f32[32,16,32,256]{3,2,1,0:T(8,128)S(1)}, f32[32,16,32,256]{3,2,1,0:T(8,128)}, u32[]{:S(2)}) copy-start(f32[32,16,32,256]{3,2,1,0:T(8,128)} %fusion.47) | copy-start | bytes 50331652
  213.7 11.1 %collective-permute-start.12 = (f32[1,16,32,256]{3,2,1,0:T(8,128)S(1)}, f32[1,16,32,256]{3,2,1,0:T(8,128)S(1)}, u32[]{:S(2)}, u32[]{:S(2)}) collective-permute-start(f32[1,16,32,256]{3,2,1,0:T(8,128)S(1)} %get-tuple-element.17), channel_id=1, source_target_pairs={{0,8},{8,16},{16,24},{1,9},{9,17},{17,25},{2,10},{10,18},{18,26},{... | collective-permute-start | bytes 1572872 | tf_op jit(solution)/shard_map/ppermute | solution.py:23
  215.3 11.2 %collective-permute-start.13 = (f32[1,16,32,256]{3,2,1,0:T(8,128)S(1)}, f32[1,16,32,256]{3,2,1,0:T(8,128)S(1)}, u32[]{:S(2)}, u32[]{:S(2)}) collective-permute-start(f32[1,16,32,256]{3,2,1,0:T(8,128)S(1)} %get-tuple-element.16), channel_id=1, source_target_pairs={{8,0},{16,8},{24,16},{9,1},{17,9},{25,17},{10,2},{18,10},{26,18},{... | collective-permute-start | bytes 1572872 | tf_op jit(solution)/shard_map/ppermute | solution.py:25
  230.7 14.2 %collective-permute-start.14 = (f32[34,16,1,256]{3,2,1,0:T(1,128)S(1)}, f32[34,16,1,256]{3,2,1,0:T(1,128)S(1)}, u32[]{:S(2)}, u32[]{:S(2)}) collective-permute-start(f32[34,16,1,256]{3,2,1,0:T(1,128)S(1)} %get-tuple-element.4), channel_id=1, source_target_pairs={{1,0},{2,1},{3,2},{4,3},{5,4},{6,5},{7,6},{9,8},{10,9},{11,10},{12... | collective-permute-start | bytes 1671176 | tf_op jit(solution)/shard_map/ppermute | solution.py:25
  232.6 13.5 %collective-permute-start.15 = (f32[34,16,1,256]{3,2,1,0:T(1,128)S(1)}, f32[34,16,1,256]{3,2,1,0:T(1,128)S(1)}, u32[]{:S(2)}, u32[]{:S(2)}) collective-permute-start(f32[34,16,1,256]{3,2,1,0:T(1,128)S(1)} %get-tuple-element.5), channel_id=1, source_target_pairs={{0,1},{1,2},{2,3},{3,4},{4,5},{5,6},{6,7},{8,9},{9,10},{10,11},{11... | collective-permute-start | bytes 1671176 | tf_op jit(solution)/shard_map/ppermute | solution.py:23
  393.5 196.5 %all-to-all-start = ((f32[8,1,524288]{2,1,0:T(1,128)}), f32[8,1,524288]{2,1,0:T(1,128)}, u32[]{:S(2)}, u32[]{:S(2)}) async-start(f32[8,1,524288]{2,1,0:T(1,128)} %reshape.8), calls=%async_computation | async-start | bytes 33554432 | tf_op jit(solution)/shard_map/all_to_all | solution.py:63
  410.8 16.5 %collective-permute-start.16 = (f32[1,16,32,256]{3,2,1,0:T(8,128)S(1)}, f32[1,16,32,256]{3,2,1,0:T(8,128)S(1)}, u32[]{:S(2)}, u32[]{:S(2)}) collective-permute-start(f32[1,16,32,256]{3,2,1,0:T(8,128)S(1)} %get-tuple-element.15), channel_id=1, source_target_pairs={{0,8},{8,16},{16,24},{1,9},{9,17},{17,25},{2,10},{10,18},{18,26},{... | collective-permute-start | bytes 1572872 | tf_op jit(solution)/shard_map/ppermute | solution.py:23
  412.1 425.9 %collective-permute-start.17 = (f32[1,16,32,256]{3,2,1,0:T(8,128)S(1)}, f32[1,16,32,256]{3,2,1,0:T(8,128)S(1)}, u32[]{:S(2)}, u32[]{:S(2)}) collective-permute-start(f32[1,16,32,256]{3,2,1,0:T(8,128)S(1)} %get-tuple-element.14), channel_id=1, source_target_pairs={{8,0},{16,8},{24,16},{9,1},{17,9},{25,17},{10,2},{18,10},{26,18},{... | collective-permute-start | bytes 1572872 | tf_op jit(solution)/shard_map/ppermute | solution.py:25
  761.9 45.3 %copy-start.7 = (f32[32,16]{1,0:T(8,128)S(1)}, f32[32,16]{1,0:T(8,128)}, u32[]{:S(2)}) copy-start(f32[32,16]{1,0:T(8,128)} %copy-done.6) | copy-start | bytes 6148
  807.1 51.6 %copy-start.9 = (f32[32,16]{1,0:T(8,128)S(1)}, f32[32,16]{1,0:T(8,128)}, u32[]{:S(2)}) copy-start(f32[32,16]{1,0:T(8,128)} %copy-done.8) | copy-start | bytes 6148
  807.1 51.6 %copy-start.12 = (f32[256,256]{1,0:T(8,128)S(1)}, f32[256,256]{1,0:T(8,128)}, u32[]{:S(2)}) copy-start(f32[256,256]{1,0:T(8,128)} %param.11) | copy-start | bytes 786436
  843.5 15.3 %collective-permute-start.18 = (f32[34,16,1,256]{3,2,1,0:T(1,128)S(1)}, f32[34,16,1,256]{3,2,1,0:T(1,128)S(1)}, u32[]{:S(2)}, u32[]{:S(2)}) collective-permute-start(f32[34,16,1,256]{3,2,1,0:T(1,128)S(1)} %get-tuple-element.2), channel_id=1, source_target_pairs={{1,0},{2,1},{3,2},{4,3},{5,4},{6,5},{7,6},{9,8},{10,9},{11,10},{12... | collective-permute-start | bytes 1671176 | tf_op jit(solution)/shard_map/ppermute | solution.py:25
  848.9 9.9 %collective-permute-start.19 = (f32[34,16,1,256]{3,2,1,0:T(1,128)S(1)}, f32[34,16,1,256]{3,2,1,0:T(1,128)S(1)}, u32[]{:S(2)}, u32[]{:S(2)}) collective-permute-start(f32[34,16,1,256]{3,2,1,0:T(1,128)S(1)} %get-tuple-element.3), channel_id=1, source_target_pairs={{0,1},{1,2},{2,3},{3,4},{4,5},{5,6},{6,7},{8,9},{9,10},{10,11},{11... | collective-permute-start | bytes 1671176 | tf_op jit(solution)/shard_map/ppermute | solution.py:23
  858.8 45.4 %copy-start.1 = (f32[256,256]{1,0:T(8,128)S(1)}, f32[256,256]{1,0:T(8,128)}, u32[]{:S(2)}) copy-start(f32[256,256]{1,0:T(8,128)} %param.10) | copy-start | bytes 786436
  (2 other events, 24.6 us)
where the time goes:
time: 922 us; the launch traced here: 905 us
  local copies, waits for them, and re-layouts  299 us (32%)
  waiting for transfers between devices  235 us (25%)
  matrix products  175 us (19%)
  other arithmetic  102 us (11%)
  starting transfers between devices  92.1 us (10%)
    all_to_all x1, waiting for transfers between devices, on_device(): lax.all_to_all(current, 'state', split_axis=3, concat_axis=2, tiled=True)  162 us
    unnamed x33, local copies, waits for them, and re-layouts  132 us
    dot_general x4, matrix products, on_device(): jnp.einsum('wrsk,tk->wrst', source, tank_inverse, precision=lax.Precision...  129 us
    all_to_all x3, local copies, waits for them, and re-layouts, on_device(): lax.all_to_all(current, 'state', split_axis=3, concat_axis=2, tiled=True)  103 us
    all_to_all x1, other arithmetic, on_device(): lax.all_to_all(current, 'state', split_axis=3, concat_axis=2, tiled=True)  59.2 us
    dot_general x1, local copies, waits for them, and re-layouts, on_device(): jnp.einsum('wrsk,tk->wrst', source, tank_inverse, precision=lax.Precision...  50.4 us
    dot_general x1, matrix products, on_device(): jnp.einsum('wrks,ts->wrkt', source, soc_inverse, precision=lax.Precision....  45.4 us
    ppermute x10, waiting for transfers between devices, extended(): lax.ppermute(tail, axis, [(i, (i + 1) % count) for i in range(ends)])  38.5 us
  transfers between devices with their start and end apart: 21, of which 17 were waited for; matrix products, arithmetic and copies ran while one was open for 24% of the time, Pallas kernels for 0%

commit v1 on v0

v1 whole, which is shorter than its diff:
```python
import functools

import jax
import jax.numpy as jnp
from jax import lax
from jax.experimental import pallas as pl
from jax.experimental.pallas import tpu as pltpu
from jax.sharding import PartitionSpec as P

ITERS = 4
HALO = ITERS
LANES = 128

step_size = 0.25
control_bound = 2.0
control_cost = 1.0
tank_spread = 0.3

MIB = 1 << 20


def split_parts(x):
    high = x.astype(jnp.bfloat16)
    low = (x - high.astype(jnp.float32)).astype(jnp.bfloat16)
    return high, low


def product(high, low, weight_high, weight_low):
    dot = functools.partial(jnp.dot, preferred_element_type=jnp.float32)
    return dot(high, weight_high) + (dot(low, weight_high) + dot(high, weight_low))


def half_shifted(slope4, price_half):
    return 0.25 * slope4 + price_half


def swap_groups(tiles, group):
    count = len(tiles)
    lane = lax.broadcasted_iota(jnp.int32, tiles[0].shape, len(tiles[0].shape) - 1)
    axis = len(tiles[0].shape) - 1
    bit = 1
    while bit < count:
        mine = (lane // group) & bit
        fresh = []
        for w in range(count):
            other = tiles[w ^ bit]
            if w & bit:
                rolled = pltpu.roll(other, LANES - bit * group, axis)
                fresh.append(jnp.where(mine != 0, tiles[w], rolled))
            else:
                rolled = pltpu.roll(other, bit * group, axis)
                fresh.append(jnp.where(mine == 0, tiles[w], rolled))
        tiles = fresh
        bit *= 2
    return tiles


def sweep_kernel(
    first_room, n, info, price, rate, v, wl, wr, sl, sr, tank, *rest
):
    chained = first_room > 0
    if chained:
        rest = rest[1:]
    out, sends = rest[0], rest[1 : 1 + n]
    base, field_a, field_b, x_high, x_low, t_high, t_low, stage = rest[1 + n :]
    planes, rows, cols = v.shape[0], v.shape[2], v.shape[3]
    wide = planes + 2 * HALO
    full = rows + 2 * HALO
    step = pl.program_id(0)
    room = first_room + step
    rooms = price.shape[0] // wide
    me = info[0]

    @pl.when(step == 0)
    def _():
        high, low = split_parts(tank[...])
        t_high[...] = high
        t_low[...] = low

    for p in range(wide):
        if p < HALO:
            base[p, :rows] = wl[p, 0]
        elif p < HALO + planes:
            base[p, :rows] = v[p - HALO, 0]
        else:
            base[p, :rows] = wr[p - HALO - planes, 0]
        base[p, rows : rows + HALO] = sr[p, 0]
        base[p, rows + HALO :] = sl[p, 0]

    source = base
    for sweep in range(ITERS):
        last = sweep == ITERS - 1
        begin = sweep + 1
        count = wide - 2 * begin
        kept = rows if last else full
        target = (field_a, field_b)[sweep % 2]

        def one(p, source=source, kept=kept):
            u = source[p]
            above = pltpu.roll(u, full - 1, 0)
            below = pltpu.roll(u, 1, 0)
            scalar = p * rooms + room
            y = (0.25 * (above - below))[:kept] + 0.5 * price[scalar]
            t = jnp.tanh(y)
            r = step_size * rate[scalar]
            near = source[p + 1, :kept] + source[p - 1, :kept]
            return (
                base[p, :kept]
                + t * (0.5 * t - y)
                + r * (near - 2.0 * u[:kept])
            )

        def pair(i, carry, begin=begin, one=one, kept=kept):
            p = begin + 2 * i
            both = jnp.concatenate([one(p), one(p + 1)], axis=0)
            high, low = split_parts(both)
            at = pl.ds(pl.multiple_of(i * (2 * kept), 16), 2 * kept)
            x_high[at, :] = high
            x_low[at, :] = low
            return carry

        lax.fori_loop(0, count // 2, pair, 0)
        pieces = 2
        per = (count // pieces) // 2 * 2
        done = 0
        for piece in range(pieces):
            size = per if piece < pieces - 1 else count - done
            at = pl.ds(done * kept, size * kept)
            u = product(x_high[at, :], x_low[at, :], t_high[...], t_low[...])
            u = u.reshape(size, kept, cols)
            if last:
                out[done : done + size, 0] = u
            else:
                target[begin + done : begin + done + size] = u
            done += size
        if not last:
            @pl.when(info[1] == 0)
            def _(target=target):
                target[HALO - 1] = jnp.zeros((full, cols), jnp.float32)

            @pl.when(info[2] == 0)
            def _(target=target):
                target[HALO + planes] = jnp.zeros((full, cols), jnp.float32)

            @pl.when(info[3] == 0)
            def _(target=target):
                target[:, rows + HALO :] = jnp.zeros((wide, HALO, cols), jnp.float32)

            @pl.when(info[4] == 0)
            def _(target=target):
                target[:, rows : rows + HALO] = jnp.zeros((wide, HALO, cols), jnp.float32)
        source = target

    width = cols // n
    per_tile = LANES // width

    def pack(g, carry):
        for tile in range(cols // LANES):
            at = slice(tile * LANES, (tile + 1) * LANES)
            tiles = [out[g * per_tile + w, 0, :, at] for w in range(per_tile)]
            tiles = swap_groups(tiles, width)
            for j in range(per_tile):
                stage[tile * per_tile + j, g] = tiles[j]
        return carry

    lax.fori_loop(0, planes // per_tile, pack, 0)
    for d in range(n):
        sends[d][0] = stage[jnp.bitwise_xor(me, d)]


def density_kernel(first_room, n, info, rate, dens, wl, wr, kl, kr, price_rows, soc, *rest):
    chained = first_room > 0
    takes = rest[:n]
    rest = rest[n:]
    if chained:
        rest = rest[1:]
    out = rest[0]
    column, level, x_high, x_low, g_high, g_low, m_high, m_low, q_high, q_low = rest[1:]
    planes, rows, cols = dens.shape[0], dens.shape[2], dens.shape[3]
    step = pl.program_id(0)
    room = first_room + step
    rooms = rate.shape[0] // planes
    me = info[0]
    per_tile = LANES // rows
    inner = takes[0].shape[2]

    @pl.when(step == 0)
    def _():
        m = soc[...]
        high, low = split_parts(m)
        m_high[...] = high
        m_low[...] = low
        line = lax.broadcasted_iota(jnp.int32, m.shape, 0)
        before = jnp.where(line == 0, 0.0, pltpu.roll(m, 1, 0))
        after = jnp.where(line == cols - 1, 0.0, pltpu.roll(m, cols - 1, 0))
        high, low = split_parts(step_size * (before - after))
        q_high[...] = high
        q_low[...] = low
        column[:8] = jnp.zeros((8, LANES), jnp.float32)
        column[8 + cols :] = jnp.zeros((8, LANES), jnp.float32)

    def group(g, carry):
        for d in range(n):
            at = pl.multiple_of(8 + inner * jnp.bitwise_xor(me, d), 8)
            column[pl.ds(at, inner)] = takes[d][0, g]
        y = 0.25 * (column[9 : 9 + cols] - column[7 : 7 + cols]) + 0.5 * price_rows[0, pl.ds(g, 1)]
        t = jnp.tanh(y).T
        for w in range(per_tile):
            p = g * per_tile + w
            here = dens[p, 0]
            level[8 : 8 + rows] = here
            level[7:8] = kl[0, pl.ds(p, 1)]
            level[8 + rows : 9 + rows] = kr[0, pl.ds(p, 1)]
            r = step_size * rate[p * rooms + room]
            lower = lax.max(p - 1, 0)
            upper = lax.min(p + 1, planes - 1)
            wind_low = jnp.where(p == 0, wl[0, 0], dens[lower, 0])
            wind_up = jnp.where(p == planes - 1, wr[0, 0], dens[upper, 0])
            tank = level[7 : 7 + rows] + level[9 : 9 + rows] - 2.0 * here
            x = here + (step_size * tank_spread) * tank + r * (wind_up + wind_low - 2.0 * here)
            at = pl.ds(pl.multiple_of(p * rows, 16), rows)
            high, low = split_parts(x)
            x_high[at, :] = high
            x_low[at, :] = low
            high, low = split_parts(t[w * rows : (w + 1) * rows] * here)
            g_high[at, :] = high
            g_low[at, :] = low
        return carry

    lax.fori_loop(0, planes // per_tile, group, 0)
    half = planes // 2
    for piece in range(2):
        at = pl.ds(piece * half * rows, half * rows)
        u = product(x_high[at, :], x_low[at, :], m_high[...], m_low[...])
        u += product(g_high[at, :], g_low[at, :], q_high[...], q_low[...])
        out[piece * half : (piece + 1) * half, 0] = u.reshape(half, rows, cols)


def smem():
    return pl.BlockSpec(memory_space=pltpu.SMEM)


def whole(shape):
    return pl.BlockSpec(shape, lambda i: (0,) * len(shape))


def room_block(planes, rows, cols, first=0):
    return pl.BlockSpec((planes, 1, rows, cols), lambda i: (0, first + i, 0, 0))


def run_sweeps(first, size, n, info, price, rate, value, halos, tank, previous):
    planes, rooms, rows, cols = value.shape
    wide, full = planes + 2 * HALO, rows + 2 * HALO
    groups = planes // (LANES // (cols // n))
    in_specs = [
        smem(),
        smem(),
        smem(),
        room_block(planes, rows, cols, first),
        room_block(HALO, rows, cols),
        room_block(HALO, rows, cols),
        room_block(wide, HALO, cols),
        room_block(wide, HALO, cols),
        whole((cols, cols)),
    ]
    args = [info, price, rate, value, *halos, tank]
    aliases = {}
    if first > 0:
        aliases = {len(args): 0}
        args.append(previous)
        in_specs.append(pl.BlockSpec(memory_space=pl.ANY))
    packed = jax.ShapeDtypeStruct((size, groups, rows, LANES), jnp.float32)
    most = (wide - 2) * full
    flops = size * 2 * 3 * most * ITERS * cols * cols
    return pl.pallas_call(
        functools.partial(sweep_kernel, first, n),
        grid=(size,),
        in_specs=in_specs,
        out_specs=[room_block(planes, rows, cols, first)]
        + [pl.BlockSpec((1, groups, rows, LANES), lambda i: (i, 0, 0, 0))] * n,
        out_shape=[jax.ShapeDtypeStruct(value.shape, jnp.float32)] + [packed] * n,
        scratch_shapes=[
            pltpu.VMEM((wide, full, cols), jnp.float32),
            pltpu.VMEM((wide, full, cols), jnp.float32),
            pltpu.VMEM((wide, full, cols), jnp.float32),
            pltpu.VMEM((most, cols), jnp.bfloat16),
            pltpu.VMEM((most, cols), jnp.bfloat16),
            pltpu.VMEM((cols, cols), jnp.bfloat16),
            pltpu.VMEM((cols, cols), jnp.bfloat16),
            pltpu.VMEM((n, groups, rows, LANES), jnp.float32),
        ],
        input_output_aliases=aliases,
        compiler_params=pltpu.CompilerParams(vmem_limit_bytes=40 * MIB),
        cost_estimate=pl.CostEstimate(
            flops=flops, bytes_accessed=size * planes * rows * cols * 12, transcendentals=size * most * ITERS * cols
        ),
        name="sweeps",
    )(*args)


def run_density(first, size, n, info, rate, density, halos, price_rows, soc, takes, previous):
    planes, rooms, rows, cols = density.shape
    groups = planes // (LANES // rows)
    inner = cols // n
    in_specs = [
        smem(),
        smem(),
        room_block(planes, rows, cols, first),
        room_block(1, rows, cols, first),
        room_block(1, rows, cols, first),
        pl.BlockSpec((1, planes, cols), lambda i: (first + i, 0, 0)),
        pl.BlockSpec((1, planes, cols), lambda i: (first + i, 0, 0)),
        pl.BlockSpec((1, groups, LANES), lambda i: (first + i, 0, 0)),
        whole((cols, cols)),
    ] + [pl.BlockSpec((1, groups, inner, LANES), lambda i: (i, 0, 0, 0))] * n
    args = [info, rate, density, *halos, price_rows, soc, *takes]
    aliases = {}
    if first > 0:
        aliases = {len(args): 0}
        args.append(previous)
        in_specs.append(pl.BlockSpec(memory_space=pl.ANY))
    most = planes * rows
    return pl.pallas_call(
        functools.partial(density_kernel, first, n),
        grid=(size,),
        in_specs=in_specs,
        out_specs=room_block(planes, rows, cols, first),
        out_shape=jax.ShapeDtypeStruct(density.shape, jnp.float32),
        scratch_shapes=[
            pltpu.VMEM((cols + 16, LANES), jnp.float32),
            pltpu.VMEM((rows + 16, cols), jnp.float32),
        ]
        + [pltpu.VMEM((most, cols), jnp.bfloat16)] * 4
        + [pltpu.VMEM((cols, cols), jnp.bfloat16)] * 4,
        input_output_aliases=aliases,
        compiler_params=pltpu.CompilerParams(vmem_limit_bytes=40 * MIB),
        cost_estimate=pl.CostEstimate(
            flops=size * 2 * 6 * most * cols * cols,
            bytes_accessed=size * most * cols * 12,
            transcendentals=size * most * cols,
        ),
        name="density",
    )(*args)


def neighbours(head, tail, axis):
    ends = lax.axis_size(axis) - 1
    before = lax.ppermute(tail, axis, [(i, i + 1) for i in range(ends)])
    after = lax.ppermute(head, axis, [(i + 1, i) for i in range(ends)])
    return before, after


def value_halos(value, first, size):
    planes, rooms, rows, cols = value.shape
    part = value[:, first : first + size]
    wl, wr = neighbours(part[:HALO], part[planes - HALO :], "wind")
    heads = jnp.concatenate([wl[:, :, :HALO], part[:, :, :HALO], wr[:, :, :HALO]], axis=0)
    at = rows - HALO
    tails = jnp.concatenate([wl[:, :, at:], part[:, :, at:], wr[:, :, at:]], axis=0)
    sl, sr = neighbours(heads, tails, "state")
    return wl, wr, sl, sr


def chunk_sizes(rooms):
    size = max(rooms // 8, 1)
    return [size] * (rooms // size)


def on_device(value_next, density, price, wind_rate, tank_inverse, soc_inverse):
    planes, rooms, rows, cols = value_next.shape
    n = lax.axis_size("state")
    me = lax.axis_index("state")
    at = lax.axis_index("wind")
    info = jnp.stack(
        [me, at, lax.axis_size("wind") - 1 - at, me, n - 1 - me]
    ).astype(jnp.int32)
    pair = jnp.stack([price, wind_rate])
    before, after = neighbours(pair[:, :HALO], pair[:, planes - HALO :], "wind")
    pair = jnp.concatenate([before, pair, after], axis=1)
    price_wide, rate_wide = pair[0].reshape(-1), pair[1].reshape(-1)
    tank, soc = tank_inverse.T, soc_inverse.T

    dwl, dwr = neighbours(density[:1], density[planes - 1 :], "wind")
    dkl, dkr = neighbours(
        jnp.swapaxes(density[:, :, 0], 0, 1), jnp.swapaxes(density[:, :, rows - 1], 0, 1), "state"
    )
    per_tile = LANES // rows
    price_rows = jnp.repeat(price.T.reshape(rooms, planes // per_tile, per_tile), rows, axis=2)
    rate_flat = wind_rate.reshape(-1)

    sizes = chunk_sizes(rooms)
    starts = [sum(sizes[:c]) for c in range(len(sizes))]
    value, density_next = None, None
    for first, size in zip(starts, sizes):
        halos = value_halos(value_next, first, size)
        value, *sends = run_sweeps(
            first, size, n, info, price_wide, rate_wide, value_next, halos, tank, value
        )
        takes = [sends[0]]
        for d in range(1, n):
            takes.append(lax.ppermute(sends[d], "state", [(i, i ^ d) for i in range(n)]))
        density_next = run_density(
            first, size, n, info, rate_flat, density, (dwl, dwr, dkl, dkr), price_rows, soc, takes, density_next
        )
    return value, density_next


def solution(mesh):
    field = P("wind", None, "state", None)
    placed = (field, field, P("wind", None), P("wind", None), P(), P())
    return jax.shard_map(
        on_device,
        mesh=mesh,
        in_specs=placed,
        out_specs=(field, field),
        check_vma=False,
    )
```

time: 922 us -> 469 us (0.51)
  the two profiles are of different devices: /device:TPU:25 before, /device:TPU:1 now
where the time goes in v1:
time: 469 us; the launch traced here: 461 us
  Pallas kernels  216 us (46%)
  starting transfers between devices  165 us (35%)
  local copies, waits for them, and re-layouts  42.4 us (9%)
  waiting for transfers between devices  21.7 us (5%)
  other arithmetic  13.5 us (3%)
    pallas_call x8, Pallas kernels, run_sweeps(): pl.pallas_call(functools.partial(sweep_kernel, first, n), grid=(size,), i...  160 us
    ppermute x19, starting transfers between devices, neighbours(): before = lax.ppermute(tail, axis, [(i, i + 1) for i in range(ends)])  78.6 us
    pallas_call x8, Pallas kernels, run_density(): pl.pallas_call(functools.partial(density_kernel, first, n), grid=(size,),...  55.9 us
    ppermute x56, starting transfers between devices, on_device(): lax.ppermute(sends[d], 'state', [(i, i ^ d) for i in range(n)])  55.8 us
    ppermute x19, starting transfers between devices, neighbours(): after = lax.ppermute(head, axis, [(i + 1, i) for i in range(ends)])  30.3 us
    unnamed x158, local copies, waits for them, and re-layouts  23.1 us
    ppermute x56, waiting for transfers between devices, on_device(): lax.ppermute(sends[d], 'state', [(i, i ^ d) for i in range(n)])  17.1 us
  transfers between devices with their start and end apart: 94, of which 6 were waited for; matrix products, arithmetic and copies ran while one was open for 7% of the time, Pallas kernels for 45%

profile of v1, /device:TPU:1, one launch (start us, length us, event | category | flops | bytes accessed | tf_op | source)
XLA Modules:
  0.0 460.8 jit_solution(4451236595769007852)
XLA Ops:
  0.7 4.1 fusion.3
  4.7 4.0 collective-permute-start.30
  16.2 4.4 fusion
  21.7 4.5 collective-permute-start.36
  26.2 5.8 %fusion.2 = (f32[32,2,4,256]{3,2,1,0:T(4,128)S(1)}, f32[32,2,4,256]{3,2,1,0:T(4,128)S(1)}, f32[32,2,4,256]{3,2,1,0:T(4,128)}, f32[32,2,4,256]{3,2,1,0:T(4,128)},...) fusion(f32[32,16,32,256]{3,2,1,0:T(8,128)} %v.15), kind=kLoop, calls=%fused_computation.23 | loop fusion | bytes 8388608 | tf_op jit(solution)/shard_map/slice | solution.py:357
  37.5 4.3 collective-permute-start.26
  43.6 4.0 collective-permute-start.22
  87.9 4.0 collective-permute-start.34
  93.3 6.2 %collective-permute-start.32 = (f32[40,2,4,256]{3,2,1,0:T(4,128)S(1)}, f32[40,2,4,256]{3,2,1,0:T(4,128)S(1)}, u32[]{:S(2)}, u32[]{:S(2)}) collective-permute-start(f32[40,2,4,256]{3,2,1,0:T(4,128)S(1)} %pad_maximum_fusion.14), channel_id=1, source_target_pairs={{0,1},{1,2},{2,3},{3,4},{4,5},{5,6},{6,7},{8,9},{9,10},{10,11},{11... | collective-permute-start | bytes 983048 | tf_op jit(solution)/shard_map/ppermute | solution.py:348
  120.3 4.5 collective-permute-start.16
  126.7 4.5 collective-permute-start.12
  140.4 4.5 collective-permute-start.8
  148.3 4.7 %collective-permute-start.4 = (f32[40,2,4,256]{3,2,1,0:T(4,128)S(1)}, f32[40,2,4,256]{3,2,1,0:T(4,128)S(1)}, u32[]{:S(2)}, u32[]{:S(2)}) collective-permute-start(f32[40,2,4,256]{3,2,1,0:T(4,128)S(1)} %pad_maximum_fusion), channel_id=1, source_target_pairs={{0,1},{1,2},{2,3},{3,4},{4,5},{5,6},{6,7},{8,9},{9,10},{10,11},{11... | collective-permute-start | bytes 983048 | tf_op jit(solution)/shard_map/ppermute | solution.py:348
  155.0 19.8 %sweeps.8 = (f32[32,16,32,256]{3,2,1,0:T(8,128)}, f32[2,8,32,128]{3,2,1,0:T(8,128)S(1)}, f32[2,8,32,128]{3,2,1,0:T(8,128)S(1)}, f32[2,8,32,128]{3,2,1,0:T(8,128)...) custom-call(s32[5]{0:T(128)S(1)} %stack.29.info, ...), custom_call_target="tpu_custom_call" | custom-call | flops 4781506560 | bytes 6291456 | tf_op jit(solution)/shard_map/sweeps/pallas_call | solution.py:275
  175.5 4.9 %collective-permute-start.88 = (f32[2,8,32,128]{3,2,1,0:T(8,128)S(1)}, f32[2,8,32,128]{3,2,1,0:T(8,128)S(1)}, u32[]{:S(2)}, u32[]{:S(2)}) collective-permute-start(f32[2,8,32,128]{3,2,1,0:T(8,128)S(1)} %get-tuple-element.140), channel_id=1, source_target_pairs={{0,2},{1,3},{2,0},{3,1},{4,6},{5,7},{6,4},{7,5},{8,10},{9,11},{10,... | collective-permute-start | bytes 786440 | tf_op jit(solution)/shard_map/ppermute | solution.py:401
  184.5 20.0 %sweeps.9 = (f32[32,16,32,256]{3,2,1,0:T(8,128)}, f32[2,8,32,128]{3,2,1,0:T(8,128)S(1)}, f32[2,8,32,128]{3,2,1,0:T(8,128)S(1)}, f32[2,8,32,128]{3,2,1,0:T(8,128)...) custom-call(s32[5]{0:T(128)S(1)} %stack.29.info, ...), custom_call_target="tpu_custom_call", output_to_operand_aliasing={{0}: (9, {})} | custom-call | flops 4781506560 | bytes 6291456 | tf_op jit(solution)/shard_map/sweeps/pallas_call | solution.py:275
  211.4 19.9 %sweeps.10 = (f32[32,16,32,256]{3,2,1,0:T(8,128)}, f32[2,8,32,128]{3,2,1,0:T(8,128)S(1)}, f32[2,8,32,128]{3,2,1,0:T(8,128)}, f32[2,8,32,128]{3,2,1,0:T(8,128)}, ...) custom-call(s32[5]{0:T(128)S(1)} %stack.29.info, ...), custom_call_target="tpu_custom_call", output_to_operand_aliasing={{0}: (9, {})} | custom-call | flops 4781506560 | bytes 6291456 | tf_op jit(solution)/shard_map/sweeps/pallas_call | solution.py:275
  245.0 8.9 %collective-permute-done.84.rest_5_ = f32[2,8,32,128]{3,2,1,0:T(8,128)} collective-permute-done((f32[2,8,32,128]{3,2,1,0:T(8,128)}, f32[2,8,32,128]{3,2,1,0:T(8,128)}, u32[]{:S(2)}, u32[]{:S(2)}) %collective-permute-start.84) | collective-permute-done | bytes 262176 | tf_op jit(solution)/shard_map/ppermute | solution.py:401
  263.2 20.2 %sweeps.11 = (f32[32,16,32,256]{3,2,1,0:T(8,128)}, f32[2,8,32,128]{3,2,1,0:T(8,128)S(1)}, f32[2,8,32,128]{3,2,1,0:T(8,128)S(1)}, f32[2,8,32,128]{3,2,1,0:T(8,128...) custom-call(s32[5]{0:T(128)S(1)} %stack.29.info, ...), custom_call_target="tpu_custom_call", output_to_operand_aliasing={{0}: (9, {})} | custom-call | flops 4781506560 | bytes 6291456 | tf_op jit(solution)/shard_map/sweeps/pallas_call | solution.py:275
  287.4 20.0 %sweeps.12 = (f32[32,16,32,256]{3,2,1,0:T(8,128)}, f32[2,8,32,128]{3,2,1,0:T(8,128)S(1)}, f32[2,8,32,128]{3,2,1,0:T(8,128)S(1)}, f32[2,8,32,128]{3,2,1,0:T(8,128...) custom-call(s32[5]{0:T(128)S(1)} %stack.29.info, ...), custom_call_target="tpu_custom_call", output_to_operand_aliasing={{0}: (9, {})} | custom-call | flops 4781506560 | bytes 6291456 | tf_op jit(solution)/shard_map/sweeps/pallas_call | solution.py:275
  312.3 19.9 %sweeps.13 = (f32[32,16,32,256]{3,2,1,0:T(8,128)}, f32[2,8,32,128]{3,2,1,0:T(8,128)S(1)}, f32[2,8,32,128]{3,2,1,0:T(8,128)S(1)}, f32[2,8,32,128]{3,2,1,0:T(8,128...) custom-call(s32[5]{0:T(128)S(1)} %stack.29.info, ...), custom_call_target="tpu_custom_call", output_to_operand_aliasing={{0}: (9, {})} | custom-call | flops 4781506560 | bytes 6291456 | tf_op jit(solution)/shard_map/sweeps/pallas_call | solution.py:275
  336.7 20.2 %sweeps.14 = (f32[32,16,32,256]{3,2,1,0:T(8,128)}, f32[2,8,32,128]{3,2,1,0:T(8,128)S(1)}, f32[2,8,32,128]{3,2,1,0:T(8,128)S(1)}, f32[2,8,32,128]{3,2,1,0:T(8,128...) custom-call(s32[5]{0:T(128)S(1)} %stack.29.info, ...), custom_call_target="tpu_custom_call", output_to_operand_aliasing={{0}: (9, {})} | custom-call | flops 4781506560 | bytes 6291456 | tf_op jit(solution)/shard_map/sweeps/pallas_call | solution.py:275
  362.4 20.0 %sweeps.15 = (f32[32,16,32,256]{3,2,1,0:T(8,128)}, f32[2,8,32,128]{3,2,1,0:T(8,128)S(1)}, f32[2,8,32,128]{3,2,1,0:T(8,128)S(1)}, f32[2,8,32,128]{3,2,1,0:T(8,128...) custom-call(s32[5]{0:T(128)S(1)} %stack.29.info, ...), custom_call_target="tpu_custom_call", output_to_operand_aliasing={{0}: (9, {})} | custom-call | flops 4781506560 | bytes 6291456 | tf_op jit(solution)/shard_map/sweeps/pallas_call | solution.py:275
  382.5 7.1 %density.8.rest_8_ = f32[32,16,32,256]{3,2,1,0:T(8,128)} custom-call(s32[5]{0:T(128)S(1)} %stack.29.info, f32[512]{0:T(512)S(1)} %reshape.13.rate, f32[32,16,32,256]{3,2,1,0:T(8,128)} %dens.15, f32[1,16,32,256]{3,2,1,0:T(8,128)S(1)} %collective-permute-done.34.wl, f32[1,16,32,256]{3,2,1,0:T(8,128)S(1)} %collective-permute-done.35.wr, ...), custom_call_target="tpu_custom_call" | custom-call | flops 1610612736 | bytes 6291456 | tf_op jit(solution)/shard_map/density/pallas_call | solution.py:323
  394.0 7.1 %density.9.rest_8_ = f32[32,16,32,256]{3,2,1,0:T(8,128)} custom-call(s32[5]{0:T(128)S(1)} %stack.29.info, f32[512]{0:T(512)S(1)} %reshape.13.rate, f32[32,16,32,256]{3,2,1,0:T(8,128)} %dens.15, f32[1,16,32,256]{3,2,1,0:T(8,128)S(1)} %collective-permute-done.34.wl, ...), custom_call_target="tpu_custom_call", output_to_operand_aliasing={{}: (17, {})} | custom-call | flops 1610612736 | bytes 6291456 | tf_op jit(solution)/shard_map/density/pallas_call | solution.py:323
  401.1 7.1 %density.10.rest_8_ = f32[32,16,32,256]{3,2,1,0:T(8,128)} custom-call(s32[5]{0:T(128)S(1)} %stack.29.info, f32[512]{0:T(512)S(1)} %reshape.13.rate, f32[32,16,32,256]{3,2,1,0:T(8,128)} %dens.15, f32[1,16,32,256]{3,2,1,0:T(8,128)S(1)} %collective-permute-done.34.wl, ...), custom_call_target="tpu_custom_call", output_to_operand_aliasing={{}: (17, {})} | custom-call | flops 1610612736 | bytes 6291456 | tf_op jit(solution)/shard_map/density/pallas_call | solution.py:323
  412.4 6.9 %density.11.rest_8_ = f32[32,16,32,256]{3,2,1,0:T(8,128)} custom-call(s32[5]{0:T(128)S(1)} %stack.29.info, f32[512]{0:T(512)S(1)} %reshape.13.rate, f32[32,16,32,256]{3,2,1,0:T(8,128)} %dens.15, f32[1,16,32,256]{3,2,1,0:T(8,128)S(1)} %collective-permute-done.34.wl, ...), custom_call_target="tpu_custom_call", output_to_operand_aliasing={{}: (17, {})} | custom-call | flops 1610612736 | bytes 6291456 | tf_op jit(solution)/shard_map/density/pallas_call | solution.py:323
  419.3 6.9 %density.12.rest_8_ = f32[32,16,32,256]{3,2,1,0:T(8,128)} custom-call(s32[5]{0:T(128)S(1)} %stack.29.info, f32[512]{0:T(512)S(1)} %reshape.13.rate, f32[32,16,32,256]{3,2,1,0:T(8,128)} %dens.15, f32[1,16,32,256]{3,2,1,0:T(8,128)S(1)} %collective-permute-done.34.wl, ...), custom_call_target="tpu_custom_call", output_to_operand_aliasing={{}: (17, {})} | custom-call | flops 1610612736 | bytes 6291456 | tf_op jit(solution)/shard_map/density/pallas_call | solution.py:323
  432.9 6.9 %density.13.rest_8_ = f32[32,16,32,256]{3,2,1,0:T(8,128)} custom-call(s32[5]{0:T(128)S(1)} %stack.29.info, f32[512]{0:T(512)S(1)} %reshape.13.rate, f32[32,16,32,256]{3,2,1,0:T(8,128)} %dens.15, f32[1,16,32,256]{3,2,1,0:T(8,128)S(1)} %collective-permute-done.34.wl, ...), custom_call_target="tpu_custom_call", output_to_operand_aliasing={{}: (17, {})} | custom-call | flops 1610612736 | bytes 6291456 | tf_op jit(solution)/shard_map/density/pallas_call | solution.py:323
  439.8 6.9 %density.14.rest_8_ = f32[32,16,32,256]{3,2,1,0:T(8,128)} custom-call(s32[5]{0:T(128)S(1)} %stack.29.info, f32[512]{0:T(512)S(1)} %reshape.13.rate, f32[32,16,32,256]{3,2,1,0:T(8,128)} %dens.15, f32[1,16,32,256]{3,2,1,0:T(8,128)S(1)} %collective-permute-done.34.wl, ...), custom_call_target="tpu_custom_call", output_to_operand_aliasing={{}: (17, {})} | custom-call | flops 1610612736 | bytes 6291456 | tf_op jit(solution)/shard_map/density/pallas_call | solution.py:323
  446.8 6.6 %collective-permute-done.42.rest_5_ = f32[2,8,32,128]{3,2,1,0:T(8,128)S(1)} collective-permute-done((f32[2,8,32,128]{3,2,1,0:T(8,128)S(1)}, f32[2,8,32,128]{3,2,1,0:T(8,128)S(1)}, u32[]{:S(2)}, u32[]{:S(2)}) %collective-permute-start.42) | collective-permute-done | bytes 262176 | tf_op jit(solution)/shard_map/ppermute | solution.py:401
  453.4 7.0 %density.15 = f32[32,16,32,256]{3,2,1,0:T(8,128)} custom-call(s32[5]{0:T(128)S(1)} %stack.29.info, f32[512]{0:T(512)S(1)} %reshape.13.rate, f32[32,16,32,256]{3,2,1,0:T(8,128)} %dens.15, f32[1,16,32,256]{3,2,1,0:T(8,128)S(1)} %collective-permute-done.34.wl, f32[1,16,32,256]{3,2,1,0:T(8,128)S(1)} %collective-permute-done.35.wr, ...), custom_call_target="tpu_custom_call", output_to_operand_aliasing={{}: (17, {})} | custom-call | flops 1610612736 | bytes 6291456 | tf_op jit(solution)/shard_map/density/pallas_call | solution.py:323
  (378 shorter events, 162.4 us)
Async XLA Ops:
  4.7 37.5 %collective-permute-start.30 = (f32[4,2,32,256]{3,2,1,0:T(8,128)}, f32[4,2,32,256]{3,2,1,0:T(8,128)S(1)}, u32[]{:S(2)}, u32[]{:S(2)}) collective-permute-start(f32[4,2,32,256]{3,2,1,0:T(8,128)} %get-tuple-element.167), channel_id=1, source_target_pairs={{0,8},{8,16},{16,24},{1,9},{9,17},{17,25},{2,10},{10,18},{18,26},{... | collective-permute-start | bytes 786440 | tf_op jit(solution)/shard_map/ppermute | solution.py:348
  8.8 34.8 %collective-permute-start.31 = (f32[4,2,32,256]{3,2,1,0:T(8,128)}, f32[4,2,32,256]{3,2,1,0:T(8,128)S(1)}, u32[]{:S(2)}, u32[]{:S(2)}) collective-permute-start(f32[4,2,32,256]{3,2,1,0:T(8,128)} %get-tuple-element.166), channel_id=1, source_target_pairs={{8,0},{16,8},{24,16},{9,1},{17,9},{25,17},{10,2},{18,10},{26,18},{... | collective-permute-start | bytes 786440 | tf_op jit(solution)/shard_map/ppermute | solution.py:349
  21.7 78.8 %collective-permute-start.36 = (f32[16,32,256]{2,1,0:T(8,128)}, f32[16,32,256]{2,1,0:T(8,128)S(1)}, u32[]{:S(2)}, u32[]{:S(2)}) collective-permute-start(f32[16,32,256]{2,1,0:T(8,128)} %bitcast.20), channel_id=1, source_target_pairs={{0,1},{1,2},{2,3},{3,4},{4,5},{5,6},{6,7},{8,9},{9,10},{10,11},{11... | collective-permute-start | bytes 1572872 | tf_op jit(solution)/shard_map/ppermute | solution.py:348
  35.6 66.8 %collective-permute-start.37 = (f32[16,32,256]{2,1,0:T(8,128)}, f32[16,32,256]{2,1,0:T(8,128)S(1)}, u32[]{:S(2)}, u32[]{:S(2)}) collective-permute-start(f32[16,32,256]{2,1,0:T(8,128)} %bitcast.37), channel_id=1, source_target_pairs={{1,0},{2,1},{3,2},{4,3},{5,4},{6,5},{7,6},{9,8},{10,9},{11,10},{12... | collective-permute-start | bytes 1572872 | tf_op jit(solution)/shard_map/ppermute | solution.py:349
  135.1 40.4 %collective-permute-start.13 = (f32[40,2,4,256]{3,2,1,0:T(4,128)S(1)}, f32[40,2,4,256]{3,2,1,0:T(4,128)S(1)}, u32[]{:S(2)}, u32[]{:S(2)}) collective-permute-start(f32[40,2,4,256]{3,2,1,0:T(4,128)S(1)} %pad_maximum_fusion.5), channel_id=1, source_target_pairs={{1,0},{2,1},{3,2},{4,3},{5,4},{6,5},{7,6},{9,8},{10,9},{11,10},{12... | collective-permute-start | bytes 983048 | tf_op jit(solution)/shard_map/ppermute | solution.py:349
  137.7 37.8 %collective-permute-start.9 = (f32[40,2,4,256]{3,2,1,0:T(4,128)S(1)}, f32[40,2,4,256]{3,2,1,0:T(4,128)S(1)}, u32[]{:S(2)}, u32[]{:S(2)}) collective-permute-start(f32[40,2,4,256]{3,2,1,0:T(4,128)S(1)} %pad_maximum_fusion.3), channel_id=1, source_target_pairs={{1,0},{2,1},{3,2},{4,3},{5,4},{6,5},{7,6},{9,8},{10,9},{11,10},{12... | collective-permute-start | bytes 983048 | tf_op jit(solution)/shard_map/ppermute | solution.py:349
  140.4 40.1 %collective-permute-start.8 = (f32[40,2,4,256]{3,2,1,0:T(4,128)S(1)}, f32[40,2,4,256]{3,2,1,0:T(4,128)S(1)}, u32[]{:S(2)}, u32[]{:S(2)}) collective-permute-start(f32[40,2,4,256]{3,2,1,0:T(4,128)S(1)} %pad_maximum_fusion.2), channel_id=1, source_target_pairs={{0,1},{1,2},{2,3},{3,4},{4,5},{5,6},{6,7},{8,9},{9,10},{10,11},{11... | collective-permute-start | bytes 983048 | tf_op jit(solution)/shard_map/ppermute | solution.py:348
  145.7 35.2 %collective-permute-start.5 = (f32[40,2,4,256]{3,2,1,0:T(4,128)S(1)}, f32[40,2,4,256]{3,2,1,0:T(4,128)S(1)}, u32[]{:S(2)}, u32[]{:S(2)}) collective-permute-start(f32[40,2,4,256]{3,2,1,0:T(4,128)S(1)} %pad_maximum_fusion.1), channel_id=1, source_target_pairs={{1,0},{2,1},{3,2},{4,3},{5,4},{6,5},{7,6},{9,8},{10,9},{11,10},{12... | collective-permute-start | bytes 983048 | tf_op jit(solution)/shard_map/ppermute | solution.py:349
  148.3 32.7 %collective-permute-start.4 = (f32[40,2,4,256]{3,2,1,0:T(4,128)S(1)}, f32[40,2,4,256]{3,2,1,0:T(4,128)S(1)}, u32[]{:S(2)}, u32[]{:S(2)}) collective-permute-start(f32[40,2,4,256]{3,2,1,0:T(4,128)S(1)} %pad_maximum_fusion), channel_id=1, source_target_pairs={{0,1},{1,2},{2,3},{3,4},{4,5},{5,6},{6,7},{8,9},{9,10},{10,11},{11... | collective-permute-start | bytes 983048 | tf_op jit(solution)/shard_map/ppermute | solution.py:348
  175.5 29.0 %collective-permute-start.88 = (f32[2,8,32,128]{3,2,1,0:T(8,128)S(1)}, f32[2,8,32,128]{3,2,1,0:T(8,128)S(1)}, u32[]{:S(2)}, u32[]{:S(2)}) collective-permute-start(f32[2,8,32,128]{3,2,1,0:T(8,128)S(1)} %get-tuple-element.140), channel_id=1, source_target_pairs={{0,2},{1,3},{2,0},{3,1},{4,6},{5,7},{6,4},{7,5},{8,10},{9,11},{10,... | collective-permute-start | bytes 786440 | tf_op jit(solution)/shard_map/ppermute | solution.py:401
  180.5 26.3 %collective-permute-start.89 = (f32[2,8,32,128]{3,2,1,0:T(8,128)S(1)}, f32[2,8,32,128]{3,2,1,0:T(8,128)S(1)}, u32[]{:S(2)}, u32[]{:S(2)}) collective-permute-start(f32[2,8,32,128]{3,2,1,0:T(8,128)S(1)} %get-tuple-element.141), channel_id=1, source_target_pairs={{0,3},{1,2},{2,1},{3,0},{4,7},{5,6},{6,5},{7,4},{8,11},{9,10},{10,... | collective-permute-start | bytes 786440 | tf_op jit(solution)/shard_map/ppermute | solution.py:401
  180.9 27.1 %collective-permute-start.90 = (f32[2,8,32,128]{3,2,1,0:T(8,128)S(1)}, f32[2,8,32,128]{3,2,1,0:T(8,128)S(1)}, u32[]{:S(2)}, u32[]{:S(2)}) collective-permute-start(f32[2,8,32,128]{3,2,1,0:T(8,128)S(1)} %get-tuple-element.142), channel_id=1, source_target_pairs={{0,4},{1,5},{2,6},{3,7},{4,0},{5,1},{6,2},{7,3},{8,12},{9,13},{10,... | collective-permute-start | bytes 786440 | tf_op jit(solution)/shard_map/ppermute | solution.py:401
  181.0 28.8 %collective-permute-start.91 = (f32[2,8,32,128]{3,2,1,0:T(8,128)S(1)}, f32[2,8,32,128]{3,2,1,0:T(8,128)S(1)}, u32[]{:S(2)}, u32[]{:S(2)}) collective-permute-start(f32[2,8,32,128]{3,2,1,0:T(8,128)S(1)} %get-tuple-element.143), channel_id=1, source_target_pairs={{0,5},{1,4},{2,7},{3,6},{4,1},{5,0},{6,3},{7,2},{8,13},{9,12},{10,... | collective-permute-start | bytes 786440 | tf_op jit(solution)/shard_map/ppermute | solution.py:401
  183.6 27.4 %collective-permute-start.92 = (f32[2,8,32,128]{3,2,1,0:T(8,128)S(1)}, f32[2,8,32,128]{3,2,1,0:T(8,128)S(1)}, u32[]{:S(2)}, u32[]{:S(2)}) collective-permute-start(f32[2,8,32,128]{3,2,1,0:T(8,128)S(1)} %get-tuple-element.144), channel_id=1, source_target_pairs={{0,6},{1,7},{2,4},{3,5},{4,2},{5,3},{6,0},{7,1},{8,14},{9,15},{10,... | collective-permute-start | bytes 786440 | tf_op jit(solution)/shard_map/ppermute | solution.py:401
  205.3 27.5 %collective-permute-start.93 = (f32[2,8,32,128]{3,2,1,0:T(8,128)S(1)}, f32[2,8,32,128]{3,2,1,0:T(8,128)S(1)}, u32[]{:S(2)}, u32[]{:S(2)}) collective-permute-start(f32[2,8,32,128]{3,2,1,0:T(8,128)S(1)} %get-tuple-element.145), channel_id=1, source_target_pairs={{0,7},{1,6},{2,5},{3,4},{4,3},{5,2},{6,1},{7,0},{8,15},{9,14},{10,... | collective-permute-start | bytes 786440 | tf_op jit(solution)/shard_map/ppermute | solution.py:401
  207.5 27.7 %collective-permute-start.80 = (f32[2,8,32,128]{3,2,1,0:T(8,128)S(1)}, f32[2,8,32,128]{3,2,1,0:T(8,128)S(1)}, u32[]{:S(2)}, u32[]{:S(2)}) collective-permute-start(f32[2,8,32,128]{3,2,1,0:T(8,128)S(1)} %get-tuple-element.131), channel_id=1, source_target_pairs={{0,1},{1,0},{2,3},{3,2},{4,5},{5,4},{6,7},{7,6},{8,9},{9,8},{10,11... | collective-permute-start | bytes 786440 | tf_op jit(solution)/shard_map/ppermute | solution.py:401
  208.7 27.5 %collective-permute-start.81 = (f32[2,8,32,128]{3,2,1,0:T(8,128)S(1)}, f32[2,8,32,128]{3,2,1,0:T(8,128)S(1)}, u32[]{:S(2)}, u32[]{:S(2)}) collective-permute-start(f32[2,8,32,128]{3,2,1,0:T(8,128)S(1)} %get-tuple-element.132), channel_id=1, source_target_pairs={{0,2},{1,3},{2,0},{3,1},{4,6},{5,7},{6,4},{7,5},{8,10},{9,11},{10,... | collective-permute-start | bytes 786440 | tf_op jit(solution)/shard_map/ppermute | solution.py:401
  210.6 27.7 %collective-permute-start.82 = (f32[2,8,32,128]{3,2,1,0:T(8,128)S(1)}, f32[2,8,32,128]{3,2,1,0:T(8,128)S(1)}, u32[]{:S(2)}, u32[]{:S(2)}) collective-permute-start(f32[2,8,32,128]{3,2,1,0:T(8,128)S(1)} %get-tuple-element.133), channel_id=1, source_target_pairs={{0,3},{1,2},{2,1},{3,0},{4,7},{5,6},{6,5},{7,4},{8,11},{9,10},{10,... | collective-permute-start | bytes 786440 | tf_op jit(solution)/shard_map/ppermute | solution.py:401
  211.0 28.4 %collective-permute-start.83 = (f32[2,8,32,128]{3,2,1,0:T(8,128)S(1)}, f32[2,8,32,128]{3,2,1,0:T(8,128)S(1)}, u32[]{:S(2)}, u32[]{:S(2)}) collective-permute-start(f32[2,8,32,128]{3,2,1,0:T(8,128)S(1)} %get-tuple-element.134), channel_id=1, source_target_pairs={{0,4},{1,5},{2,6},{3,7},{4,0},{5,1},{6,2},{7,3},{8,12},{9,13},{10,... | collective-permute-start | bytes 786440 | tf_op jit(solution)/shard_map/ppermute | solution.py:401
  253.9 29.5 %collective-permute-start.75 = (f32[2,8,32,128]{3,2,1,0:T(8,128)}, f32[2,8,32,128]{3,2,1,0:T(8,128)S(1)}, u32[]{:S(2)}, u32[]{:S(2)}) collective-permute-start(f32[2,8,32,128]{3,2,1,0:T(8,128)} %copy-done.72), channel_id=1, source_target_pairs={{0,3},{1,2},{2,1},{3,0},{4,7},{5,6},{6,5},{7,4},{8,11},{9,10},{10,... | collective-permute-start | bytes 786440 | tf_op jit(solution)/shard_map/ppermute | solution.py:401
  254.5 29.3 %collective-permute-start.76 = (f32[2,8,32,128]{3,2,1,0:T(8,128)}, f32[2,8,32,128]{3,2,1,0:T(8,128)S(1)}, u32[]{:S(2)}, u32[]{:S(2)}) collective-permute-start(f32[2,8,32,128]{3,2,1,0:T(8,128)} %copy-done.71), channel_id=1, source_target_pairs={{0,4},{1,5},{2,6},{3,7},{4,0},{5,1},{6,2},{7,3},{8,12},{9,13},{10,... | collective-permute-start | bytes 786440 | tf_op jit(solution)/shard_map/ppermute | solution.py:401
  255.6 28.6 %collective-permute-start.77 = (f32[2,8,32,128]{3,2,1,0:T(8,128)}, f32[2,8,32,128]{3,2,1,0:T(8,128)S(1)}, u32[]{:S(2)}, u32[]{:S(2)}) collective-permute-start(f32[2,8,32,128]{3,2,1,0:T(8,128)} %copy-done.70), channel_id=1, source_target_pairs={{0,5},{1,4},{2,7},{3,6},{4,1},{5,0},{6,3},{7,2},{8,13},{9,12},{10,... | collective-permute-start | bytes 786440 | tf_op jit(solution)/shard_map/ppermute | solution.py:401
  256.9 28.7 %collective-permute-start.78 = (f32[2,8,32,128]{3,2,1,0:T(8,128)}, f32[2,8,32,128]{3,2,1,0:T(8,128)S(1)}, u32[]{:S(2)}, u32[]{:S(2)}) collective-permute-start(f32[2,8,32,128]{3,2,1,0:T(8,128)} %copy-done.69), channel_id=1, source_target_pairs={{0,6},{1,7},{2,4},{3,5},{4,2},{5,3},{6,0},{7,1},{8,14},{9,15},{10,... | collective-permute-start | bytes 786440 | tf_op jit(solution)/shard_map/ppermute | solution.py:401
  258.4 28.3 %collective-permute-start.79 = (f32[2,8,32,128]{3,2,1,0:T(8,128)}, f32[2,8,32,128]{3,2,1,0:T(8,128)S(1)}, u32[]{:S(2)}, u32[]{:S(2)}) collective-permute-start(f32[2,8,32,128]{3,2,1,0:T(8,128)} %copy-done.68), channel_id=1, source_target_pairs={{0,7},{1,6},{2,5},{3,4},{4,3},{5,2},{6,1},{7,0},{8,15},{9,14},{10,... | collective-permute-start | bytes 786440 | tf_op jit(solution)/shard_map/ppermute | solution.py:401
  284.2 25.9 %collective-permute-start.68 = (f32[2,8,32,128]{3,2,1,0:T(8,128)S(1)}, f32[2,8,32,128]{3,2,1,0:T(8,128)S(1)}, u32[]{:S(2)}, u32[]{:S(2)}) collective-permute-start(f32[2,8,32,128]{3,2,1,0:T(8,128)S(1)} %get-tuple-element.117), channel_id=1, source_target_pairs={{0,3},{1,2},{2,1},{3,0},{4,7},{5,6},{6,5},{7,4},{8,11},{9,10},{10,... | collective-permute-start | bytes 786440 | tf_op jit(solution)/shard_map/ppermute | solution.py:401
  310.7 26.0 %collective-permute-start.61 = (f32[2,8,32,128]{3,2,1,0:T(8,128)S(1)}, f32[2,8,32,128]{3,2,1,0:T(8,128)S(1)}, u32[]{:S(2)}, u32[]{:S(2)}) collective-permute-start(f32[2,8,32,128]{3,2,1,0:T(8,128)S(1)} %get-tuple-element.109), channel_id=1, source_target_pairs={{0,3},{1,2},{2,1},{3,0},{4,7},{5,6},{6,5},{7,4},{8,11},{9,10},{10,... | collective-permute-start | bytes 786440 | tf_op jit(solution)/shard_map/ppermute | solution.py:401
  333.8 25.5 %collective-permute-start.64 = (f32[2,8,32,128]{3,2,1,0:T(8,128)S(1)}, f32[2,8,32,128]{3,2,1,0:T(8,128)S(1)}, u32[]{:S(2)}, u32[]{:S(2)}) collective-permute-start(f32[2,8,32,128]{3,2,1,0:T(8,128)S(1)} %get-tuple-element.112), channel_id=1, source_target_pairs={{0,6},{1,7},{2,4},{3,5},{4,2},{5,3},{6,0},{7,1},{8,14},{9,15},{10,... | collective-permute-start | bytes 786440 | tf_op jit(solution)/shard_map/ppermute | solution.py:401
  357.0 32.6 %collective-permute-start.53 = (f32[2,8,32,128]{3,2,1,0:T(8,128)S(1)}, f32[2,8,32,128]{3,2,1,0:T(8,128)S(1)}, u32[]{:S(2)}, u32[]{:S(2)}) collective-permute-start(f32[2,8,32,128]{3,2,1,0:T(8,128)S(1)} %get-tuple-element.100), channel_id=1, source_target_pairs={{0,2},{1,3},{2,0},{3,1},{4,6},{5,7},{6,4},{7,5},{8,10},{9,11},{10,... | collective-permute-start | bytes 786440 | tf_op jit(solution)/shard_map/ppermute | solution.py:401
  357.6 33.4 %collective-permute-start.54 = (f32[2,8,32,128]{3,2,1,0:T(8,128)S(1)}, f32[2,8,32,128]{3,2,1,0:T(8,128)S(1)}, u32[]{:S(2)}, u32[]{:S(2)}) collective-permute-start(f32[2,8,32,128]{3,2,1,0:T(8,128)S(1)} %get-tuple-element.101), channel_id=1, source_target_pairs={{0,3},{1,2},{2,1},{3,0},{4,7},{5,6},{6,5},{7,4},{8,11},{9,10},{10,... | collective-permute-start | bytes 786440 | tf_op jit(solution)/shard_map/ppermute | solution.py:401
  359.3 31.7 %collective-permute-start.55 = (f32[2,8,32,128]{3,2,1,0:T(8,128)S(1)}, f32[2,8,32,128]{3,2,1,0:T(8,128)S(1)}, u32[]{:S(2)}, u32[]{:S(2)}) collective-permute-start(f32[2,8,32,128]{3,2,1,0:T(8,128)S(1)} %get-tuple-element.102), channel_id=1, source_target_pairs={{0,4},{1,5},{2,6},{3,7},{4,0},{5,1},{6,2},{7,3},{8,12},{9,13},{10,... | collective-permute-start | bytes 786440 | tf_op jit(solution)/shard_map/ppermute | solution.py:401
  360.1 31.4 %collective-permute-start.56 = (f32[2,8,32,128]{3,2,1,0:T(8,128)S(1)}, f32[2,8,32,128]{3,2,1,0:T(8,128)S(1)}, u32[]{:S(2)}, u32[]{:S(2)}) collective-permute-start(f32[2,8,32,128]{3,2,1,0:T(8,128)S(1)} %get-tuple-element.103), channel_id=1, source_target_pairs={{0,5},{1,4},{2,7},{3,6},{4,1},{5,0},{6,3},{7,2},{8,13},{9,12},{10,... | collective-permute-start | bytes 786440 | tf_op jit(solution)/shard_map/ppermute | solution.py:401
  360.5 32.6 %collective-permute-start.57 = (f32[2,8,32,128]{3,2,1,0:T(8,128)S(1)}, f32[2,8,32,128]{3,2,1,0:T(8,128)S(1)}, u32[]{:S(2)}, u32[]{:S(2)}) collective-permute-start(f32[2,8,32,128]{3,2,1,0:T(8,128)S(1)} %get-tuple-element.104), channel_id=1, source_target_pairs={{0,6},{1,7},{2,4},{3,5},{4,2},{5,3},{6,0},{7,1},{8,14},{9,15},{10,... | collective-permute-start | bytes 786440 | tf_op jit(solution)/shard_map/ppermute | solution.py:401
  (138 other events, 2365.5 us)
